TPU v7x, 256 devices: a whole 4x4x8 slice. The times are simulated.
256 devices in a mesh: los: 32 (over x, z), sky: 8 (over y, core).
Axes of the slice: x: 4, y: 4, z: 8, core: 2. Of those that a mesh axis runs over, the one named last changes fastest.
Arguments:
- potentials: bfloat16 [128, 128, 4096], P('los', 'sky'), may hold values from -6 to 6
- shell_weight: float32 [128], P('los'), may hold values from 0.004 to 0.02
- shell_dist: float32 [128], P('los'), may hold values from 1 to 6.12, as said below
- source_dist: float32 [128], P('los'), may hold values from 1 to 6.12, as said below
Outputs:
- convergence: bfloat16 [128, 128, 4096], P('los', 'sky')
- shear_one: bfloat16 [128, 128, 4096], P('los', 'sky')
- shear_two: bfloat16 [128, 128, 4096], P('los', 'sky')
Inputs may be any that keep to these rules, and one draw needn't show every extreme that they name: shell_dist rises strictly with the shell index. source_dist[s] lies strictly between shell_dist[s] and shell_dist[s + 1].
All inputs are finite; a program needn't handle non-finite values.
Results may differ from a plain program's by a relative error of at most 0.001.
Values may be sent and summed in bfloat16 or wider, within the bound.
No kernel may reach another device: no remote copies, remote signals or barrier semaphores. Data moves between devices by JAX's collectives and lax.ppermute only.
A program may use at most 64 MiB of HBM per device.

v0:
```python
import jax
import jax.numpy as jnp
from jax import lax
from jax.sharding import PartitionSpec as P


def with_halo(cells, sides, width):
    for axis, dim in sides:
        count = lax.axis_size(axis)
        head = lax.slice_in_dim(cells, 0, width, axis=dim)
        tail = lax.slice_in_dim(cells, cells.shape[dim] - width, cells.shape[dim], axis=dim)
        cells = jnp.concatenate(
            [
                lax.ppermute(tail, axis, [(i, (i + 1) % count) for i in range(count)]),
                cells,
                lax.ppermute(head, axis, [((i + 1) % count, i) for i in range(count)]),
            ],
            axis=dim,
        )
    return cells


def first_cols(field):
    return (
        jnp.roll(field, 2, axis=-1)
        - 8.0 * jnp.roll(field, 1, axis=-1)
        + 8.0 * jnp.roll(field, -1, axis=-1)
        - jnp.roll(field, -2, axis=-1)
    ) / 12.0


def second_cols(field):
    return (
        -jnp.roll(field, 2, axis=-1)
        + 16.0 * jnp.roll(field, 1, axis=-1)
        - 30.0 * field
        + 16.0 * jnp.roll(field, -1, axis=-1)
        - jnp.roll(field, -2, axis=-1)
    ) / 12.0


def first_rows(padded, height):
    return (
        padded[:, 0:height, :]
        - 8.0 * padded[:, 1 : height + 1, :]
        + 8.0 * padded[:, 3 : height + 3, :]
        - padded[:, 4 : height + 4, :]
    ) / 12.0


def second_rows(padded, height):
    return (
        -padded[:, 0:height, :]
        + 16.0 * padded[:, 1 : height + 1, :]
        - 30.0 * padded[:, 2 : height + 2, :]
        + 16.0 * padded[:, 3 : height + 3, :]
        - padded[:, 4 : height + 4, :]
    ) / 12.0


def local_sums(potential, near_weight, far_weight):
    field = potential.astype(jnp.float32)
    local_near = jnp.cumsum(near_weight[:, None, None] * field, axis=0)
    local_far = jnp.cumsum(far_weight[:, None, None] * field, axis=0)
    return (local_near, local_far)


def nearer_sums(total_near, total_far):
    stacked = jnp.stack((total_near, total_far))[None]
    received = lax.all_to_all(stacked, "los", split_axis=3, concat_axis=0, tiled=True)
    earlier = jnp.cumsum(received, axis=0) - received
    result = lax.all_to_all(earlier, "los", split_axis=0, concat_axis=3, tiled=True)
    return (result[0, 0], result[0, 1])


def lens_from(local_near, local_far, prefix, source_dist):
    running_near = prefix[0][None] + local_near
    running_far = prefix[1][None] + local_far
    return running_near - running_far / source_dist[:, None, None]


def on_device(potentials, shell_weight, shell_dist, source_dist):
    height = potentials.shape[1]
    near_weight = shell_weight * shell_dist
    far_weight = near_weight * shell_dist
    local_near, local_far = local_sums(potentials, near_weight, far_weight)
    prefix = nearer_sums(local_near[-1], local_far[-1])
    lens_map = lens_from(local_near, local_far, prefix, source_dist)
    padded = with_halo(lens_map, (("sky", 1),), 2)
    interior = padded[:, 2 : height + 2, :]
    second_x = second_cols(interior)
    second_y = second_rows(padded, height)
    cross = first_rows(first_cols(padded), height)
    convergence = (0.5 * (second_x + second_y)).astype(jnp.bfloat16)
    shear_one = (0.5 * (second_x - second_y)).astype(jnp.bfloat16)
    shear_two = cross.astype(jnp.bfloat16)
    return (convergence, shear_one, shear_two)


def solution(mesh):
    return jax.shard_map(
        on_device,
        mesh=mesh,
        in_specs=(P("los", "sky", None), P("los"), P("los"), P("los")),
        out_specs=(P("los", "sky", None), P("los", "sky", None), P("los", "sky", None)),
        check_vma=False,
    )
```

profile of v0, /device:TPU:32, one launch (start us, length us, event | category | flops | bytes accessed | tf_op | source)
XLA Modules:
  0.0 103.1 jit_solution(17439832646547839495)
XLA Ops:
  0.6 0.7 fusion.27
  1.4 1.2 %fusion.2 = f32[4,16,4096]{2,1,0:T(8,128)S(1)} fusion(bf16[4,16,4096]{2,1,0:T(8,128)(2,1)} %param.4, f32[4]{0:T(128)S(1)} %get-tuple-element.15), kind=kOutput, calls=%fused_computation.15 | output fusion | flops 1310720 | bytes 1572880 | tf_op jit(solution)/shard_map/jit(cumsum)/reduce_window_sum | solution.py:64
  2.9 4.4 %copy.83 = f32[1,2,16,4096]{2,1,0,3:T(2,128)} copy(f32[1,2,16,4096]{3,2,1,0:T(8,128)S(1)} %maximum_bitcast_fusion) | data formatting | bytes 1048576 | tf_op jit(solution)/shard_map/broadcast_in_dim | solution.py:69
  7.2 7.3 %reshape.11 = f32[32,1,4096]{2,1,0:T(1,128)S(1)} reshape(f32[4096,1,2,16]{3,2,1,0:T(2,128)} %bitcast.18) | data formatting | bytes 1048576
  14.6 28.6 %all_to_all.36 = f32[32,1,4096]{2,1,0:T(1,128)S(1)} all-to-all(f32[32,1,4096]{2,1,0:T(1,128)S(1)} %reshape.11), channel_id=1, replica_groups=mesh['los'=32,'sky'=8] {'los'}, dimensions={0} | all-to-all | bytes 1048576 | tf_op jit(solution)/shard_map/all_to_all | solution.py:70
  43.2 0.5 broadcast.48
  43.7 1.9 %reduce = f32[32,4096]{1,0:T(8,128)S(1)} reduce(f32[32,1,4096]{2,1,0:T(1,128)S(1)} %all_to_all.36, f32[]{:T(128)} %broadcast.48), dimensions={1}, to_apply=%all_to_all.26.reduce_sub_computation | reduce | bytes 1048580 | tf_op jit(solution)/shard_map/all_to_all | solution.py:70
  45.6 6.9 %reshape.12 = f32[4096,1,2,16]{3,2,1,0:T(2,128)} reshape(f32[32,4096]{1,0:T(8,128)S(1)} %reduce) | data formatting | bytes 1048576
  52.5 5.1 %copy.85 = f32[1,2,16,32,128]{4,2,1,3,0:T(8,128)S(1)} copy(f32[1,2,16,32,128]{2,1,4,3,0:T(2,128)} %bitcast.19) | data formatting | bytes 1048576 | tf_op jit(solution)/shard_map/all_to_all | solution.py:70
  57.6 4.1 %reduce-window_subtract_fusion = f32[32,2,16,128]{3,2,1,0:T(8,128)S(1)} fusion(f32[1,2,16,32,128]{4,2,1,3,0:T(8,128)S(1)} %copy.85), kind=kOutput, calls=%fused_computation.47 | output fusion | flops 4194304 | bytes 1048576 | tf_op jit(solution)/shard_map/jit(cumsum)/reduce_window_sum | solution.py:71
  61.7 21.6 %all_to_all.37 = f32[32,2,16,128]{3,2,1,0:T(8,128)S(1)} all-to-all(f32[32,2,16,128]{3,2,1,0:T(8,128)S(1)} %reduce-window_subtract_fusion), channel_id=1, replica_groups=mesh['los'=32,'sky'=8] {'los'}, dimensions={0} | all-to-all | bytes 1048576 | tf_op jit(solution)/shard_map/all_to_all | solution.py:72
  84.8 0.4 fusion.33
  85.1 0.4 fusion.35
  85.7 0.5 collective-permute-start
  86.3 5.2 %collective-permute-done = f32[4,2,4096]{2,0,1:T(4,128)S(1)} collective-permute-done((f32[4,2,4096]{2,0,1:T(4,128)S(1)}, f32[4,2,4096]{2,0,1:T(4,128)S(1)}, u32[]{:S(2)}, u32[]{:S(2)}) %collective-permute-start) | collective-permute-done | bytes 131104 | tf_op jit(solution)/shard_map/ppermute | solution.py:14
  91.5 0.7 copy_dynamic-update-slice_fusion
  92.4 0.8 fusion.31
  93.2 0.8 fusion.28
  94.4 0.4 pad_maximum_fusion
  94.8 1.4 %maximum_subtract_fusion = f32[4,20,4096]{2,0,1:T(4,128)S(1)} fusion(f32[4,20,4094]{2,0,1:T(4,128)S(1)} %get-tuple-element.23, f32[4,20,2]{2,0,1:T(4,128)S(1)} %get-tuple-element.21, f32[4,20,4095]{2,0,1:T(4,128)S(1)} %get-tuple-element.18, f32[4,20,1]{2,0,1:T(4,128)S(1)} %get-tuple-element.20), kind=kLoop, calls=%fused_computation.10 | loop fusion | flops 1310720 | bytes 3932160 | tf_op jit(solution)/shard_map/sub | solution.py:25
  96.2 2.3 %fusion = f32[4,20,4096]{2,1,0:T(8,128)S(1)} fusion(f32[4,20,4096]{2,0,1:T(4,128)S(1)} %pad_maximum_fusion.1, f32[4,20,4096]{2,0,1:T(4,128)S(1)} %maximum_subtract_fusion, f32[4,20,4096]{2,0,1:T(4,128)S(1)} %pad_maximum_fusion), kind=kLoop, calls=%fused_computation.5 | loop fusion | flops 1310720 | bytes 5242880 | tf_op jit(solution)/shard_map/div | solution.py:24
  98.5 1.2 %fusion.13 = bf16[4,16,4096]{2,1,0:T(8,128)(2,1)} fusion(f32[4,20,4096]{2,1,0:T(8,128)S(1)} %fusion), kind=kLoop, calls=%fused_computation.27 | loop fusion | flops 1835008 | bytes 4718592 | tf_op jit(solution)/shard_map/convert_element_type | solution.py:96
  100.0 2.2 %multiply_convert_fusion = (bf16[4,16,4096]{2,1,0:T(8,128)(2,1)}, f32[4,16,4096]{2,1,0:T(8,128)S(1)}, f32[4,16,4096]{2,1,0:T(8,128)S(1)}) fusion(f32[4,2,4096]{2,1,0:T(2,128)S(1)} %copy.90, f32[4,16,4096]{2,1,0:T(8,128)S(1)} %divide_subtract_fusion, f32[4,2,4096]{2,1,0:T(2,128)S(1)} %copy.88, f32[4,16,2]{2,1,0:T(8,128)S(1)} %get-tuple-element.26, ...), kind=kLoop, calls=%fused_computation.44 | loop fusion | flops 7340032 | bytes 8126464 | tf_op jit(solution)/shard_map/convert_element_type | solution.py:95
  102.2 0.9 multiply_convert_fusion.1
  (26 shorter events, 2.7 us)
Async XLA Ops:
  0.6 2.0 %copy-start = (bf16[4,16,4096]{2,1,0:T(8,128)(2,1)S(1)}, bf16[4,16,4096]{2,1,0:T(8,128)(2,1)}, u32[]{:S(2)}) copy-start(bf16[4,16,4096]{2,1,0:T(8,128)(2,1)} %param.4) | copy-start | bytes 1572868
  83.6 0.7 copy-start.1
  85.6 6.7 %collective-permute-start.1 = (f32[4,2,4096]{2,0,1:T(4,128)S(1)}, f32[4,2,4096]{2,0,1:T(4,128)S(1)}, u32[]{:S(2)}, u32[]{:S(2)}) collective-permute-start(f32[4,2,4096]{2,0,1:T(4,128)S(1)} %copy.89), channel_id=1, source_target_pairs={{1,0},{2,1},{3,2},{4,3},{5,4},{6,5},{7,6},{0,7},{9,8},{10,9},{11,1... | collective-permute-start | bytes 393224 | tf_op jit(solution)/shard_map/ppermute | solution.py:16
  85.7 5.8 %collective-permute-start = (f32[4,2,4096]{2,0,1:T(4,128)S(1)}, f32[4,2,4096]{2,0,1:T(4,128)S(1)}, u32[]{:S(2)}, u32[]{:S(2)}) collective-permute-start(f32[4,2,4096]{2,0,1:T(4,128)S(1)} %copy.87), channel_id=1, source_target_pairs={{0,1},{1,2},{2,3},{3,4},{4,5},{5,6},{6,7},{7,0},{8,9},{9,10},{10,1... | collective-permute-start | bytes 393224 | tf_op jit(solution)/shard_map/ppermute | solution.py:14
where the time goes:
time: 103 us
  blocking collectives  50.2 us (49%)
  local copies, waits for them, and re-layouts  29.1 us (28%)
  other arithmetic  17.2 us (17%)
  waiting for transfers between devices  5.2 us (5%)
    all_to_all x1, blocking collectives, nearer_sums(): lax.all_to_all(stacked, 'los', split_axis=3, concat_axis=0, tiled=True)  28.6 us
    all_to_all x1, blocking collectives, nearer_sums(): lax.all_to_all(earlier, 'los', split_axis=0, concat_axis=3, tiled=True)  21.6 us
    unnamed x9, local copies, waits for them, and re-layouts  15.6 us
    all_to_all x2, local copies, waits for them, and re-layouts, nearer_sums(): lax.all_to_all(stacked, 'los', split_axis=3, concat_axis=0, tiled=True)  5.62 us
    ppermute x1, waiting for transfers between devices, with_halo(): lax.ppermute(tail, axis, [(i, (i + 1) % count) for i in range(count)])  5.2 us
    broadcast_in_dim x1, local copies, waits for them, and re-layouts, nearer_sums(): stacked = jnp.stack((total_near, total_far))[None]  4.39 us
    another operation x1, other arithmetic, nearer_sums(): earlier = jnp.cumsum(received, axis=0) - received  4.06 us
    div x1, other arithmetic, first_cols(): (jnp.roll(field, 2, axis=-1) - 8.0 * jnp.roll(field, 1, axis=-1) + 8.0 *...  2.3 us
  transfers between devices with their start and end apart: 2, of which 1 were waited for; matrix products, arithmetic and copies ran while one was open for 1% of the time, Pallas kernels for 0%

commit v1 on v0

--- a/solution.py
+++ b/solution.py
@@ -2,6 +2,7 @@
 import jax.numpy as jnp
 from jax import lax
 from jax.sharding import PartitionSpec as P
+from jax.lax import all_to_all, axis_size
 
 
 def with_halo(cells, sides, width):
@@ -66,8 +67,15 @@
 
 
 def nearer_sums(total_near, total_far):
+
+    def supply_pools_for(chunk):
+        w_next = jnp.split(chunk, axis_size("los"), 3)
+        heard = all_to_all(jnp.stack(w_next, axis=0), axis_name="los", split_axis=0, concat_axis=0)
+        y1 = jnp.concatenate(heard, 0)
+        return y1
+
     stacked = jnp.stack((total_near, total_far))[None]
-    received = lax.all_to_all(stacked, "los", split_axis=3, concat_axis=0, tiled=True)
+    received = supply_pools_for(stacked)
     earlier = jnp.cumsum(received, axis=0) - received
     result = lax.all_to_all(earlier, "los", split_axis=0, concat_axis=3, tiled=True)
     return (result[0, 0], result[0, 1])

time: 103 us -> 74 us (0.72); the launches traced: 103 us -> 72.6 us
  local copies, waits for them, and re-layouts: 29.1 us -> 2.86 us
  other arithmetic: 17.2 us -> 13 us
  waiting for transfers between devices: 5.2 us -> 2.57 us
  starting transfers between devices: 0.52 us -> 2.96 us
    unnamed x9 -> x36, local copies, waits for them, and re-layouts: 15.6 us -> 0.46 us
    all_to_all x2 -> x0, local copies, waits for them, and re-layouts: 5.62 us -> none  [nearer_sums(): lax.all_to_all(stacked, 'los', split_axis=3, concat_axis=0, tiled=True)]
    broadcast_in_dim x1 -> x0, local copies, waits for them, and re-layouts: 4.39 us -> none  [nearer_sums(): stacked = jnp.stack((total_near, total_far))[None]]
    ppermute x1, starting transfers between devices: 0.02 us -> 2.96 us  [with_halo(): lax.ppermute(head, axis, [((i + 1) % count, i) for i in range(count)])]
    ppermute x1, waiting for transfers between devices: 5.2 us -> 2.57 us  [with_halo(): lax.ppermute(tail, axis, [(i, (i + 1) % count) for i in range(count)])]
    all_to_all x1 -> x0, other arithmetic: 1.89 us -> none  [nearer_sums(): lax.all_to_all(stacked, 'los', split_axis=3, concat_axis=0, tiled=True)]
    sub x1 -> x0, other arithmetic: 1.42 us -> none  [first_cols(): jnp.roll(field, 2, axis=-1) - 8.0 * jnp.roll(field, 1, axis=-1)]
    another operation x1, other arithmetic: 1.2 us -> 0.16 us  [local_sums(): local_far = jnp.cumsum(far_weight[:, None, None] * field, axis=0)]
  transfers between devices with their start and end apart: 2 -> 2, of which waited for: 1 -> 1; matrix products, arithmetic and copies ran while one was open for 1% -> 0% of each run, Pallas kernels for 0% -> 0%
where the time goes in v1:
time: 74 us; the launch traced here: 72.6 us
  blocking collectives  50.2 us (68%)
  other arithmetic  13 us (18%)
  starting transfers between devices  2.96 us (4%)
  local copies, waits for them, and re-layouts  2.86 us (4%)
  waiting for transfers between devices  2.57 us (3%)
  between operations  1 us (1%)
    all_to_all x1, blocking collectives, supply_pools_for(): all_to_all(jnp.stack(w_next, axis=0), axis_name='los', split_axis=0, conc...  28.6 us
    all_to_all x1, blocking collectives, nearer_sums(): lax.all_to_all(earlier, 'los', split_axis=0, concat_axis=3, tiled=True)  21.6 us
    another operation x1, other arithmetic, nearer_sums(): earlier = jnp.cumsum(received, axis=0) - received  3.97 us
    ppermute x1, starting transfers between devices, with_halo(): lax.ppermute(head, axis, [((i + 1) % count, i) for i in range(count)])  2.96 us
    ppermute x1, waiting for transfers between devices, with_halo(): lax.ppermute(tail, axis, [(i, (i + 1) % count) for i in range(count)])  2.57 us
    convert_element_type x1, other arithmetic, on_device(): shear_one = (0.5 * (second_x - second_y)).astype(jnp.bfloat16)  2.22 us
    div x1, other arithmetic, first_cols(): (jnp.roll(field, 2, axis=-1) - 8.0 * jnp.roll(field, 1, axis=-1) + 8.0 *...  2.01 us
  transfers between devices with their start and end apart: 2, of which 1 were waited for; matrix products, arithmetic and copies ran while one was open for 0% of the time, Pallas kernels for 0%

profile of v1, /device:TPU:32, one launch (start us, length us, event | category | flops | bytes accessed | tf_op | source)
XLA Modules:
  0.0 72.6 jit_solution(3506243648050748723)
XLA Ops:
  0.6 0.7 %fusion.36 = (f32[4]{0:T(128)S(1)}, f32[4]{0:T(128)S(1)}) fusion(f32[4]{0:T(128)} %param.6, f32[4]{0:T(128)} %param.5), kind=kLoop, calls=%fused_computation.128 | loop fusion | flops 8 | bytes 64 | tf_op jit(solution)/shard_map/mul | solution.py:93
  1.4 1.2 %fusion.10 = f32[4,16,4096]{2,1,0:T(8,128)S(1)} fusion(bf16[4,16,4096]{2,1,0:T(8,128)(2,1)} %param.4, f32[4]{0:T(128)S(1)} %get-tuple-element.7), kind=kOutput, calls=%fused_computation.25 | output fusion | flops 1310720 | bytes 1572880 | tf_op jit(solution)/shard_map/jit(cumsum)/reduce_window_sum | solution.py:64
  2.6 0.2 fusion.11
  2.8 0.1 maximum_bitcast_fusion
  3.3 28.6 %all_to_all.23 = f32[32,1,2,16,128]{4,3,2,1,0:T(8,128)S(1)} all-to-all(f32[32,1,2,16,128]{4,3,2,1,0:T(8,128)S(1)} %constant_dynamic-update-slice_fusion), channel_id=1, replica_groups=mesh['los'=32,'sky'=8] {'los'}, dimensions={0} | all-to-all | bytes 1048576 | tf_op jit(solution)/shard_map/all_to_all | solution.py:73
  31.9 4.0 %reduce-window_subtract_fusion = f32[32,2,16,128]{3,2,1,0:T(8,128)S(1)} fusion(f32[32,1,2,16,128]{4,3,2,1,0:T(8,128)S(1)} %all_to_all.23), kind=kOutput, calls=%fused_computation.57 | output fusion | flops 4194304 | bytes 1048576 | tf_op jit(solution)/shard_map/jit(cumsum)/reduce_window_sum | solution.py:79
  35.9 21.6 %all_to_all.24 = f32[32,2,16,128]{3,2,1,0:T(8,128)S(1)} all-to-all(f32[32,2,16,128]{3,2,1,0:T(8,128)S(1)} %reduce-window_subtract_fusion), channel_id=1, replica_groups=mesh['los'=32,'sky'=8] {'los'}, dimensions={0} | all-to-all | bytes 1048576 | tf_op jit(solution)/shard_map/all_to_all | solution.py:80
  57.5 0.3 copy.70
  57.8 0.3 copy_bitcast_fusion
  58.1 0.3 divide_subtract_fusion
  58.4 0.1 fusion.43
  58.5 0.3 fusion.40
  58.9 0.4 fusion.42
  59.3 0.1 fusion.39
  59.3 3.0 %collective-permute-start.1 = (f32[4,2,4096]{2,1,0:T(2,128)S(1)}, f32[4,2,4096]{2,1,0:T(2,128)S(1)}, u32[]{:S(2)}, u32[]{:S(2)}) collective-permute-start(f32[4,2,4096]{2,1,0:T(2,128)S(1)} %get-tuple-element.21), channel_id=1, source_target_pairs={{1,0},{2,1},{3,2},{4,3},{5,4},{6,5},{7,6},{0,7},{9,8},{10,9},{11,1... | collective-permute-start | bytes 393224 | tf_op jit(solution)/shard_map/ppermute | solution.py:17
  62.3 0.1 fusion.41
  62.4 2.6 %collective-permute-done = f32[4,2,4096]{2,1,0:T(2,128)S(1)} collective-permute-done((f32[4,2,4096]{2,1,0:T(2,128)S(1)}, f32[4,2,4096]{2,1,0:T(2,128)S(1)}, u32[]{:S(2)}, u32[]{:S(2)}) %collective-permute-start) | collective-permute-done | bytes 131104 | tf_op jit(solution)/shard_map/ppermute | solution.py:15
  64.9 0.2 pad_maximum_fusion.8
  65.2 0.5 fusion.38
  65.7 0.5 fusion.37
  66.2 2.0 %fusion.2 = f32[4,20,4096]{2,1,0:T(8,128)S(1)} fusion(f32[4,2,4096]{2,1,0:T(2,128)S(1)} %collective-permute-done.1, f32[4,16,4096]{2,1,0:T(8,128)S(1)} %divide_subtract_fusion, f32[4,2,4096]{2,1,0:T(2,128)S(1)} %collective-permute-done, f32[4,20,4094]{2,1,0:T(8,128)S(1)} %get-tuple-element.9, f32[4,20,4095]{2,1,0:T(8,128)S(1)} %get-tuple-element.11, ...), kind=kLoop, calls=%fused_computation.3 | loop fusion | flops 5898240 | bytes 7862400 | tf_op jit(solution)/shard_map/div | solution.py:25
  68.3 1.2 %fusion.22 = bf16[4,16,4096]{2,1,0:T(8,128)(2,1)} fusion(f32[4,20,4096]{2,1,0:T(8,128)S(1)} %fusion.2), kind=kLoop, calls=%fused_computation.38 | loop fusion | flops 1835008 | bytes 4718592 | tf_op jit(solution)/shard_map/convert_element_type | solution.py:104
  69.5 2.2 %multiply_convert_fusion = (bf16[4,16,4096]{2,1,0:T(8,128)(2,1)}, f32[4,16,4096]{2,1,0:T(8,128)S(1)}, f32[4,16,4096]{2,1,0:T(8,128)S(1)}) fusion(f32[4,2,4096]{2,1,0:T(2,128)S(1)} %collective-permute-done.1, f32[4,16,4096]{2,1,0:T(8,128)S(1)} %divide_subtract_fusion, f32[4,2,4096]{2,1,0:T(2,128)S(1)} %collective-permute-done, ...), kind=kLoop, calls=%fused_computation.54 | loop fusion | flops 7340032 | bytes 8126464 | tf_op jit(solution)/shard_map/convert_element_type | solution.py:103
  71.7 0.9 %multiply_convert_fusion.1 = bf16[4,16,4096]{2,1,0:T(8,128)(2,1)} fusion(f32[4,16,4096]{2,1,0:T(8,128)S(1)} %get-tuple-element.5, f32[4,16,4096]{2,1,0:T(8,128)S(1)} %get-tuple-element.4), kind=kLoop, calls=%fused_computation.55 | loop fusion | flops 786432 | bytes 2621440 | tf_op jit(solution)/shard_map/convert_element_type | solution.py:102
  (41 shorter events, 0.2 us)
Async XLA Ops:
  0.6 2.0 %copy-start = (bf16[4,16,4096]{2,1,0:T(8,128)(2,1)S(1)}, bf16[4,16,4096]{2,1,0:T(8,128)(2,1)}, u32[]{:S(2)}) copy-start(bf16[4,16,4096]{2,1,0:T(8,128)(2,1)} %param.4) | copy-start | bytes 1572868
  57.5 0.7 copy-start.1
  59.3 5.6 %collective-permute-start = (f32[4,2,4096]{2,1,0:T(2,128)S(1)}, f32[4,2,4096]{2,1,0:T(2,128)S(1)}, u32[]{:S(2)}, u32[]{:S(2)}) collective-permute-start(f32[4,2,4096]{2,1,0:T(2,128)S(1)} %get-tuple-element.20), channel_id=1, source_target_pairs={{0,1},{1,2},{2,3},{3,4},{4,5},{5,6},{6,7},{7,0},{8,9},{9,10},{10,1... | collective-permute-start | bytes 393224 | tf_op jit(solution)/shard_map/ppermute | solution.py:15
  59.3 5.6 %collective-permute-start.1 = (f32[4,2,4096]{2,1,0:T(2,128)S(1)}, f32[4,2,4096]{2,1,0:T(2,128)S(1)}, u32[]{:S(2)}, u32[]{:S(2)}) collective-permute-start(f32[4,2,4096]{2,1,0:T(2,128)S(1)} %get-tuple-element.21), channel_id=1, source_target_pairs={{1,0},{2,1},{3,2},{4,3},{5,4},{6,5},{7,6},{0,7},{9,8},{10,9},{11,1... | collective-permute-start | bytes 393224 | tf_op jit(solution)/shard_map/ppermute | solution.py:17
